TPU v7x, 32 devices: a whole 2x2x4 slice. The times are simulated.
32 devices in a mesh: grp: 2 (over y), col: 8 (over z, x), row: 2 (over core).
Axes of the slice: x: 2, y: 2, z: 4, core: 2. Of those that a mesh axis runs over, the one named last changes fastest.
Arguments:
- genotypes: float32 [6, 12288, 256], P(None, ('grp', 'col', 'row')), parts along dimension 1, may hold values from -1 to 2, as said below
- prior_slab: float32 [1536, 6144], P(('grp', 'row'), 'col'), parts along dimension 0, may hold values from -6 to 6
Outputs:
- updated_slab: float32 [1536, 6144], P(('grp', 'row'), 'col'), parts along dimension 0
There are 2 independent parts, one for each index of `grp`. A program takes and returns all parts, laid end to end along the dimension named above; each array names one. Nothing has to cross between parts.
Inputs may be any that keep to these rules, and one draw needn't show every extreme that they name: `genotypes`: each variant has its own allele frequency, which drifts with the sample index; about one call in twenty is missing (value -1), and in every block one variant has no called sample at all.
All inputs are finite; a program needn't handle non-finite values.
Results may differ from a plain program's by a relative error of at most 0.0003.
Values sent between devices are 32-bit elements; how exact they have to be, the bound alone decides.
A program may use at most 64 MiB of HBM per device.

v0:
```python
import jax
import jax.numpy as jnp
from jax import lax
from jax.sharding import PartitionSpec as P


def broadcast(shard, axis, root):
    mine = lax.axis_index(axis) == root
    return lax.psum(jnp.where(mine, shard, jnp.zeros_like(shard)), axis)


def standardize(values, center, spread):
    called = values >= 0
    dosage = jnp.where(called, values, 0.0)
    return jnp.where(called, (dosage - center) / spread, 0.0)


def per_device(genotypes, prior_slab):
    called = genotypes >= 0
    dosage = jnp.where(called, genotypes, 0.0)
    local_sums = (
        jnp.sum(dosage, axis=1),
        jnp.sum(dosage * dosage, axis=1),
        jnp.sum(called.astype(jnp.float32), axis=1),
    )
    allele_sum, square_sum, counts = lax.psum(
        (local_sums[0], local_sums[1], local_sums[2]), ("col", "row")
    )
    counts = jnp.maximum(counts, 1.0)
    center = allele_sum / counts
    spread = jnp.sqrt(jnp.maximum(square_sum / counts - center * center, 0.05))
    block_count = genotypes.shape[0]
    factor = 1.0 / jnp.sqrt(jnp.float32(block_count * genotypes.shape[2]))
    row_calls = broadcast(genotypes, "col", 0)
    row_values = standardize(row_calls, center[:, None, :], spread[:, None, :])
    column_values = standardize(
        lax.all_gather(genotypes, "row", axis=1, tiled=True), center[:, None, :], spread[:, None, :]
    )
    accumulated = jnp.einsum(
        "kiv,kjv->ij", row_values, column_values, precision=lax.Precision.HIGHEST
    )
    return prior_slab + accumulated * factor


def solution(mesh):
    placed = (P(None, ("grp", "col", "row"), None), P(("grp", "row"), "col"))
    return jax.shard_map(
        per_device, mesh=mesh, in_specs=placed, out_specs=P(("grp", "row"), "col"), check_vma=False
    )
```

profile of v0, /device:TPU:0, one launch (start us, length us, event | category | flops | bytes accessed | tf_op | source)
XLA Modules:
  0.0 142.0 jit_solution(1609809066220572419)
XLA Ops:
  7.4 0.0 all-reduce.3.cloned.1.call-start
  7.4 3.7 %fusion.9 = (f32[6,256]{1,0:T(8,128)S(1)}, f32[6,256]{1,0:T(8,128)S(1)}, f32[6,256]{1,0:T(8,128)S(1)}, f32[6,384,256]{2,1,0:T(8,128)}) fusion(f32[6,384,256]{2,1,0:T(8,128)} %param.2, pred[]{:T(512)S(6)} %eq.3), kind=kLoop, calls=%fused_computation.16 | loop fusion | flops 4713984 | bytes 4737025 | tf_op jit(solution)/shard_map/reduce_sum | solution.py:22
  11.1 0.0 copy-start
  11.1 0.0 all-reduce.3.cloned.1.call-update
  11.1 0.0 all-gather.2.cloned.1.call-start
  11.2 0.5 all-gather.2.cloned.1.call-update
  11.7 65.1 %all-reduce = (f32[6,256]{1,0:T(8,128)S(1)}, f32[6,256]{1,0:T(8,128)S(1)}, f32[6,256]{1,0:T(8,128)S(1)}) all-reduce(f32[6,256]{1,0:T(8,128)S(1)} %get-tuple-element.6, f32[6,256]{1,0:T(8,128)S(1)} %get-tuple-element.7, f32[6,256]{1,0:T(8,128)S(1)} %get-tuple-element.5), channel_id=1, replica_groups=mesh['grp'=2,'col'=8,'row'=2] {'col','row'}, use_global_device_ids=true, to_apply=%region_6.7 | all-reduce | flops 4608 | bytes 36864 | tf_op jit(solution)/shard_map/psum | solution.py:26
  76.8 46.9 %all-reduce.3.cloned.1.call-done = f32[6,384,256]{2,1,0:T(8,128)} async-done(((f32[6,384,256]{2,1,0:T(8,128)}), f32[6,384,256]{2,1,0:T(8,128)}) %all-reduce.3.cloned.1.call-update) | async-done | bytes 2359312 | tf_op jit(solution)/shard_map/psum | solution.py:9
  123.7 0.0 all-gather.2.cloned.1.call-done
  123.8 0.0 copy-done
  123.8 10.8 %fusion.12 = f32[384,768]{1,0:T(8,128)} fusion(f32[384,768]{1,0:T(8,128)S(1)} %copy-done, f32[6,768,256]{2,1,0:T(8,128)} %all-gather.2.cloned.1.call-done, f32[6,256]{1,0:T(8,128)S(1)} %get-tuple-element.13, f32[6,256]{1,0:T(8,128)S(1)} %get-tuple-element.12, f32[6,384,256]{2,1,0:T(8,128)} %all-reduce.3.cloned.1.call-done), kind=kOutput, calls=%fused_computation.19 | convolution fusion | flops 5445255168 | bytes 9449472 | tf_op jit(solution)/shard_map/kiv,kjv->ij/dot_general | solution.py:39
  (1 shorter events, 0.0 us)
Async XLA Ops:
  7.4 116.4 %all-reduce.3.cloned.1.call-start = ((), (), s32[]{:S(2)}) async-start(), calls=%async_computation | async-start | bytes 4718592 | tf_op jit(solution)/shard_map/psum | solution.py:9
  11.1 112.7 %copy-start = (f32[384,768]{1,0:T(8,128)S(1)}, f32[384,768]{1,0:T(8,128)}, u32[]{:S(2)}) copy-start(f32[384,768]{1,0:T(8,128)} %param.3) | copy-start | bytes 3538948
  11.1 112.6 %all-gather.2.cloned.1.call-start = ((), (), s32[]{:S(2)}) async-start(), calls=%async_computation.1 | async-start | bytes 7077888 | tf_op jit(solution)/shard_map/all_gather | solution.py:37
Sparse Core Ops, SparseCore 0:
  11.8 111.9 all-reduce.2
Sparse Core Ops, SparseCore 1:
  13.1 17.0 all-gather.1
where the time goes:
time: 142 us
  blocking collectives  65.1 us (46%)
  waiting for transfers between devices  47.5 us (33%)
  between operations  14.8 us (10%)
  matrix products  10.8 us (8%)
  other arithmetic  3.74 us (3%)
    psum x1, blocking collectives, per_device(): lax.psum((local_sums[0], local_sums[1], local_sums[2]), ('col', 'row'))  65.1 us
    psum x1, waiting for transfers between devices, broadcast(): return lax.psum(jnp.where(mine, shard, jnp.zeros_like(shard)), axis)  46.9 us
    dot_general x1, matrix products, per_device(): jnp.einsum('kiv,kjv->ij', row_values, column_values, precision=lax.Precis...  10.8 us
    reduce_sum x1, other arithmetic, per_device(): jnp.sum(dosage, axis=1)  3.73 us
  transfers between devices with their start and end apart: 2, of which 1 were waited for; matrix products, arithmetic and copies ran while one was open for 0% of the time, Pallas kernels for 0%

commit v1 on v0

v1 whole, which is shorter than its diff:
```python
import functools
import math

import jax
import jax.numpy as jnp
from jax import lax
from jax.experimental import pallas as pl
from jax.experimental.pallas import tpu as pltpu
from jax.sharding import PartitionSpec as P

MESH = pl.DeviceIdType.MESH
PIECES = 4
SKEW = 2
WINDOW = 3


def grid_of(count):
    fast = 2 ** (int(math.log2(count)) // 2)
    return count // fast, fast


def split(values):
    high = values.astype(jnp.bfloat16)
    return high, (values - high.astype(jnp.float32)).astype(jnp.bfloat16)


def kernel(slow_n, fast_n, calls_hbm, prior_hbm, out_ref, own, other, rows, high_t, low_t,
           sums, sums_in, scaling, local_sem, pair_send, pair_recv, stat_send, stat_recv,
           piece_send, piece_recv):
    blocks, samples, variants = own.shape
    stages = sums_in.shape[0]
    piece = samples // PIECES
    pieces = blocks * PIECES
    depth_max = max(slow_n + fast_n - 2, fast_n + 1, slow_n + 1)

    grp, col, row = lax.axis_index("grp"), lax.axis_index("col"), lax.axis_index("row")
    z, x = col // fast_n, col % fast_n
    first, second = jnp.where(row == 0, z, x), jnp.where(row == 0, x, z)
    first_n = jnp.where(row == 0, slow_n, fast_n)
    second_n = jnp.where(row == 0, fast_n, slow_n)

    def device(a, b):
        return (grp, jnp.where(row == 0, a * fast_n + b, b * fast_n + a), row)

    is_root = col == 0
    on_edge = jnp.logical_and(first == 0, second > 0)
    on_spine = second == 0
    depth = jnp.where(on_edge, second + 2, first + second)
    parent = device(
        jnp.where(on_edge, 1, jnp.where(on_spine, jnp.maximum(first - 1, 0), first)),
        jnp.where(on_edge, second, jnp.where(on_spine, 0, second - 1)),
    )
    has_a = jnp.logical_and(
        jnp.logical_not(on_edge),
        jnp.where(on_spine, first + 1 < first_n, second + 1 < second_n),
    )
    child_a = device(
        jnp.where(on_spine, jnp.minimum(first + 1, first_n - 1), first),
        jnp.where(on_spine, 0, jnp.minimum(second + 1, second_n - 1)),
    )
    has_b = jnp.where(on_spine, first >= 1, first == 1)
    child_b = device(jnp.where(on_spine, first, 0), jnp.where(on_spine, 1, second))

    pair = (grp, col, 1 - row)

    def partner(stage):
        if stage == 0:
            return pair
        bit = 2 ** (stage - 1)
        return (grp, col + bit - 2 * bit * ((col // bit) % 2), row)

    own_copy = pltpu.make_async_copy(calls_hbm, own, local_sem.at[0])
    own_copy.start()
    prior_copy = pltpu.make_async_copy(prior_hbm, out_ref, local_sem.at[1])
    prior_copy.start()
    root_copy = pltpu.make_async_copy(calls_hbm, rows, local_sem.at[2])

    barrier = pltpu.get_barrier_semaphore()
    for stage in range(stages):
        pl.semaphore_signal(barrier, inc=1, device_id=partner(stage), device_id_type=MESH)

    @pl.when(jnp.logical_not(is_root))
    def _():
        pl.semaphore_signal(barrier, inc=1, device_id=parent, device_id_type=MESH)

    @pl.when(has_a)
    def _():
        pl.semaphore_signal(barrier, inc=1, device_id=child_a, device_id_type=MESH)

    @pl.when(has_b)
    def _():
        pl.semaphore_signal(barrier, inc=1, device_id=child_b, device_id_type=MESH)

    greeted = (stages + jnp.where(is_root, 0, 1) + jnp.where(has_a, 1, 0) + jnp.where(has_b, 1, 0))
    pl.semaphore_wait(barrier, greeted)

    def part(ref, c):
        return ref.at[c // PIECES, pl.ds(pl.multiple_of((c % PIECES) * piece, piece), piece)]

    def from_root(c):
        return pltpu.make_async_remote_copy(
            src_ref=part(calls_hbm, c), dst_ref=part(rows, c), send_sem=piece_send.at[0, c],
            recv_sem=piece_recv.at[c], device_id=child_a, device_id_type=MESH)

    def forward(c, which, target):
        return pltpu.make_async_remote_copy(
            src_ref=part(rows, c), dst_ref=part(rows, c), send_sem=piece_send.at[which, c],
            recv_sem=piece_recv.at[c], device_id=target, device_id_type=MESH)

    def pair_copy(k):
        return pltpu.make_async_remote_copy(
            src_ref=calls_hbm.at[k], dst_ref=other.at[k], send_sem=pair_send.at[k],
            recv_sem=pair_recv.at[k], device_id=pair, device_id_type=MESH)

    def stat_copy(stage):
        return pltpu.make_async_remote_copy(
            src_ref=sums.at[stage], dst_ref=sums_in.at[stage], send_sem=stat_send.at[stage],
            recv_sem=stat_recv.at[stage], device_id=partner(stage), device_id_type=MESH)

    @pl.when(is_root)
    def _():
        for c in range(min(WINDOW, pieces)):
            from_root(c).start()
        root_copy.start()

    own_copy.wait()

    def local_sums(k, carry):
        values = own[k]
        called = values >= 0
        dosage = jnp.where(called, values, 0.0)
        sums[0, 0, pl.ds(k, 1), :] = jnp.sum(dosage, axis=0, keepdims=True)
        sums[0, 1, pl.ds(k, 1), :] = jnp.sum(dosage * dosage, axis=0, keepdims=True)
        sums[0, 2, pl.ds(k, 1), :] = jnp.sum(jnp.where(called, 1.0, 0.0), axis=0, keepdims=True)
        return carry

    lax.fori_loop(0, blocks, local_sums, 0)
    stat_copy(0).start()

    @pl.when(is_root)
    def _():
        root_copy.wait()

    prior_copy.wait()

    stat_slots = [1 + 2 * stage for stage in range(stages)]
    prep_slot = stat_slots[-1] + 1
    lag = max(SKEW * (depth_max - 1), prep_slot + 1 - (PIECES - 1))
    slots = lag + pieces
    factor = 1.0 / math.sqrt(blocks * variants)

    def standardize(values, k):
        center, scale = scaling[0, pl.ds(k, 1), :], scaling[1, pl.ds(k, 1), :]
        return jnp.where(values >= 0, (values - center) * scale, 0.0)

    def slot(s, carry):
        c = s - SKEW * (depth - 1)
        in_range = jnp.logical_and(c >= 0, c < pieces)

        @pl.when(jnp.logical_and(in_range, jnp.logical_not(is_root)))
        def _():
            forward(c, 0, parent).wait_recv()

            @pl.when(has_a)
            def _():
                forward(c, 0, child_a).start()

            @pl.when(has_b)
            def _():
                forward(c, 1, child_b).start()

        @pl.when(jnp.logical_and(is_root, s < pieces))
        def _():
            from_root(s).wait_send()

            @pl.when(s + WINDOW < pieces)
            def _():
                from_root(s + WINDOW).start()

        for stage, at in enumerate(stat_slots):
            @pl.when(s == at)
            def _():
                stat_copy(stage).wait_recv()
                total = sums[stage] + sums_in[stage]
                sums[stage + 1] = total
                if stage + 1 < stages:
                    stat_copy(stage + 1).start()
                else:
                    counts = jnp.maximum(total[2], 1.0)
                    center = total[0] / counts
                    spread = jnp.sqrt(jnp.maximum(total[1] / counts - center * center, 0.05))
                    scaling[0] = center
                    scaling[1] = 1.0 / spread

        @pl.when(jnp.logical_and(s >= 1, s < 1 + blocks))
        def _():
            pair_copy(s - 1).start()

        @pl.when(jnp.logical_and(s >= prep_slot, s < prep_slot + blocks))
        def _():
            k = s - prep_slot
            pair_copy(k).wait_recv()
            for held, place in ((own, row), (other, 1 - row)):
                for at in range(0, samples, 128):
                    scores = standardize(held[k, at:at + 128, :], k) * factor
                    high, low = split(scores.T)
                    lanes = pl.ds(pl.multiple_of(place * samples + at, 128), 128)
                    high_t[k, :, lanes] = high
                    low_t[k, :, lanes] = low

        @pl.when(jnp.logical_and(s >= lag + PIECES - 1, (s - lag) % PIECES == PIECES - 1))
        def _():
            k = (s - lag) // PIECES
            high, low = split(standardize(rows[k], k))

            def tile(n, carry):
                lanes = pl.ds(pl.multiple_of(n * 256, 256), 256)
                right_high, right_low = high_t[k, :, lanes], low_t[k, :, lanes]
                dot = functools.partial(jnp.dot, preferred_element_type=jnp.float32)
                out_ref[:, lanes] += (
                    dot(high, right_high) + (dot(low, right_high) + dot(high, right_low)))
                return carry

            lax.fori_loop(0, out_ref.shape[1] // 256, tile, 0)

        return carry

    lax.fori_loop(0, slots, slot, 0)

    for stage in range(stages):
        stat_copy(stage).wait_send()

    def drain_pair(k, carry):
        pair_copy(k).wait_send()
        return carry

    lax.fori_loop(0, blocks, drain_pair, 0)

    def drain(c, carry):
        @pl.when(jnp.logical_and(has_a, jnp.logical_not(is_root)))
        def _():
            forward(c, 0, child_a).wait_send()

        @pl.when(has_b)
        def _():
            forward(c, 1, child_b).wait_send()

        return carry

    lax.fori_loop(0, pieces, drain, 0)


def per_device(slow_n, fast_n, genotypes, prior_slab):
    blocks, samples, variants = genotypes.shape
    height, width = prior_slab.shape
    stages = 1 + int(math.log2(slow_n * fast_n))
    pieces = blocks * PIECES
    return pl.pallas_call(
        functools.partial(kernel, slow_n, fast_n),
        out_shape=jax.ShapeDtypeStruct((height, width), jnp.float32),
        in_specs=[pl.BlockSpec(memory_space=pl.ANY)] * 2,
        out_specs=pl.BlockSpec(memory_space=pltpu.VMEM),
        scratch_shapes=[
            pltpu.VMEM((blocks, samples, variants), jnp.float32),
            pltpu.VMEM((blocks, samples, variants), jnp.float32),
            pltpu.VMEM((blocks, samples, variants), jnp.float32),
            pltpu.VMEM((blocks, variants, width), jnp.bfloat16),
            pltpu.VMEM((blocks, variants, width), jnp.bfloat16),
            pltpu.VMEM((stages + 1, 3, blocks, variants), jnp.float32),
            pltpu.VMEM((stages, 3, blocks, variants), jnp.float32),
            pltpu.VMEM((2, blocks, variants), jnp.float32),
            pltpu.SemaphoreType.DMA((3,)),
            pltpu.SemaphoreType.DMA((blocks,)),
            pltpu.SemaphoreType.DMA((blocks,)),
            pltpu.SemaphoreType.DMA((stages,)),
            pltpu.SemaphoreType.DMA((stages,)),
            pltpu.SemaphoreType.DMA((2, pieces)),
            pltpu.SemaphoreType.DMA((pieces,)),
        ],
        compiler_params=pltpu.CompilerParams(
            collective_id=0, has_side_effects=True, vmem_limit_bytes=48 * 2**20),
        cost_estimate=pl.CostEstimate(
            flops=6 * height * width * blocks * variants,
            bytes_accessed=4 * (2 * blocks * samples * variants + 2 * height * width),
            transcendentals=0),
    )(genotypes, prior_slab)


def solution(mesh):
    slow_n, fast_n = grid_of(mesh.shape["col"])
    placed = (P(None, ("grp", "col", "row"), None), P(("grp", "row"), "col"))
    return jax.shard_map(
        functools.partial(per_device, slow_n, fast_n), mesh=mesh, in_specs=placed,
        out_specs=P(("grp", "row"), "col"), check_vma=False
    )
```

time: 142 us -> 50 us (0.35)
  the two profiles are of different devices: /device:TPU:0 before, /device:TPU:26 now
where the time goes in v1:
time: 50 us; the launch traced here: 49.9 us
  Pallas kernels  45.9 us (92%)
  local copies, waits for them, and re-layouts  3.95 us (8%)
    pallas_call x1, Pallas kernels, per_device(): pl.pallas_call(functools.partial(kernel, slow_n, fast_n), out_shape=jax.S...  45.9 us
    unnamed x5, local copies, waits for them, and re-layouts  3.95 us

profile of v1, /device:TPU:26, one launch (start us, length us, event | category | flops | bytes accessed | tf_op | source)
XLA Modules:
  0.0 49.9 jit_solution(4172841563927954484)
XLA Ops:
  0.0 0.0 copy-start
  0.0 1.7 %copy-done = f32[6,384,256]{2,1,0:T(8,128)S(1)} copy-done((f32[6,384,256]{2,1,0:T(8,128)S(1)}, f32[6,384,256]{2,1,0:T(8,128)}, u32[]{:S(2)}) %copy-start) | copy-done | bytes 2359320
  1.7 0.0 copy-start.1
  1.7 1.3 %copy-done.1 = f32[384,768]{1,0:T(8,128)S(1)} copy-done((f32[384,768]{1,0:T(8,128)S(1)}, f32[384,768]{1,0:T(8,128)}, u32[]{:S(2)}) %copy-start.1) | copy-done | bytes 1179672
  2.9 45.9 %shard_map.28 = f32[384,768]{1,0:T(8,128)S(1)} custom-call(f32[6,384,256]{2,1,0:T(8,128)S(1)} %copy-done, f32[384,768]{1,0:T(8,128)S(1)} %copy-done.1), custom_call_target="tpu_custom_call" | custom-call | flops 2717908992 | bytes 7077888 | tf_op jit(solution)/shard_map/pallas_call | solution.py:258
  48.9 1.0 %copy.4 = f32[384,768]{1,0:T(8,128)} copy(f32[384,768]{1,0:T(8,128)S(1)} %shard_map.28) | data formatting | bytes 2359296
Async XLA Ops:
  0.0 1.7 %copy-start = (f32[6,384,256]{2,1,0:T(8,128)S(1)}, f32[6,384,256]{2,1,0:T(8,128)}, u32[]{:S(2)}) copy-start(f32[6,384,256]{2,1,0:T(8,128)} %calls_hbm.1) | copy-start | bytes 7077892
  1.7 1.3 %copy-start.1 = (f32[384,768]{1,0:T(8,128)S(1)}, f32[384,768]{1,0:T(8,128)}, u32[]{:S(2)}) copy-start(f32[384,768]{1,0:T(8,128)} %prior_hbm.1) | copy-start | bytes 3538948

commit v2 on v1

v2 whole, which is shorter than its diff:
```python
import functools
import math

import jax
import jax.numpy as jnp
from jax import lax
from jax.experimental import pallas as pl
from jax.experimental.pallas import tpu as pltpu
from jax.sharding import PartitionSpec as P

MESH = pl.DeviceIdType.MESH
PIECES = 8
WINDOW = 8
GATHERED = 7
TOTALLED = 10
VMEM_MIB = 52


def grid_of(count):
    fast = 2 ** (int(math.log2(count)) // 2)
    return count // fast, fast


def split(values):
    high = values.astype(jnp.bfloat16)
    return high, (values - high.astype(jnp.float32)).astype(jnp.bfloat16)


def kernel(slow_n, fast_n, calls_hbm, out_ref, own, other, rows, high, low, row_high, row_low,
           sums, gathered, joined, joined_in, totals, scaling, local_sem, pair_send, pair_recv,
           sums_send, sums_recv, joined_sem, totals_send, totals_recv, piece_send, piece_recv):
    blocks, samples, variants = own.shape
    columns = gathered.shape[0]
    piece = samples // PIECES
    pieces = blocks * PIECES
    arrival = TOTALLED + WINDOW

    grp, col, row = lax.axis_index("grp"), lax.axis_index("col"), lax.axis_index("row")
    z, x = col // fast_n, col % fast_n
    first, second = jnp.where(row == 0, z, x), jnp.where(row == 0, x, z)
    first_n = jnp.where(row == 0, slow_n, fast_n)
    second_n = jnp.where(row == 0, fast_n, slow_n)

    def device(a, b):
        return (grp, jnp.where(row == 0, a * fast_n + b, b * fast_n + a), row)

    is_root = col == 0
    on_edge = jnp.logical_and(first == 0, second > 0)
    on_spine = second == 0
    parent = device(
        jnp.where(on_edge, 1, jnp.where(on_spine, jnp.maximum(first - 1, 0), first)),
        jnp.where(on_edge, second, jnp.where(on_spine, 0, second - 1)),
    )
    has_a = jnp.logical_and(
        jnp.logical_not(on_edge),
        jnp.where(on_spine, first + 1 < first_n, second + 1 < second_n),
    )
    child_a = device(
        jnp.where(on_spine, jnp.minimum(first + 1, first_n - 1), first),
        jnp.where(on_spine, 0, jnp.minimum(second + 1, second_n - 1)),
    )
    has_b = jnp.where(on_spine, first >= 1, first == 1)
    child_b = device(jnp.where(on_spine, first, 0), jnp.where(on_spine, 1, second))

    pair = (grp, col, 1 - row)

    root = (grp, 0, row)

    own_copy = pltpu.make_async_copy(calls_hbm, own, local_sem.at[0])
    own_copy.start()
    root_copy = pltpu.make_async_copy(calls_hbm, rows, local_sem.at[1])

    barrier = pltpu.get_barrier_semaphore()
    pl.semaphore_signal(barrier, inc=1, device_id=pair, device_id_type=MESH)

    @pl.when(jnp.logical_not(is_root))
    def _():
        pl.semaphore_signal(barrier, inc=1, device_id=parent, device_id_type=MESH)

    @pl.when(is_root)
    def _():
        def greet(j, carry):
            pl.semaphore_signal(barrier, inc=1, device_id=(grp, j, row), device_id_type=MESH)
            return carry

        lax.fori_loop(1, columns, greet, 0)

    pl.semaphore_wait(
        barrier,
        1 + jnp.where(is_root, 0, 1) + jnp.where(has_a, 1, 0) + jnp.where(has_b, 1, 0))

    def part(ref, c):
        return ref.at[c // PIECES, pl.ds(pl.multiple_of((c % PIECES) * piece, piece), piece)]

    def from_root(c):
        return pltpu.make_async_remote_copy(
            src_ref=part(calls_hbm, c), dst_ref=part(rows, c), send_sem=piece_send.at[0, c],
            recv_sem=piece_recv.at[c], device_id=child_a, device_id_type=MESH)

    def forward(c, which, target):
        return pltpu.make_async_remote_copy(
            src_ref=part(rows, c), dst_ref=part(rows, c), send_sem=piece_send.at[which, c],
            recv_sem=piece_recv.at[c], device_id=target, device_id_type=MESH)

    def pair_copy(k):
        return pltpu.make_async_remote_copy(
            src_ref=calls_hbm.at[k], dst_ref=other.at[k], send_sem=pair_send.at[k],
            recv_sem=pair_recv.at[k], device_id=pair, device_id_type=MESH)

    def sums_copy(j):
        return pltpu.make_async_remote_copy(
            src_ref=sums, dst_ref=gathered.at[j], send_sem=sums_send, recv_sem=sums_recv.at[j],
            device_id=root, device_id_type=MESH)

    joined_copy = pltpu.make_async_remote_copy(
        src_ref=joined, dst_ref=joined_in, send_sem=joined_sem.at[0], recv_sem=joined_sem.at[1],
        device_id=pair, device_id_type=MESH)

    def totals_copy(which, target):
        return pltpu.make_async_remote_copy(
            src_ref=totals, dst_ref=totals, send_sem=totals_send.at[which], recv_sem=totals_recv,
            device_id=target, device_id_type=MESH)

    @pl.when(is_root)
    def _():
        for c in range(min(WINDOW, pieces)):
            from_root(c).start()
        root_copy.start()

    own_copy.wait()

    def local_sums(k, carry):
        values = own[k]
        called = values >= 0
        dosage = jnp.where(called, values, 0.0)
        sums[0, pl.ds(k, 1), :] = jnp.sum(dosage, axis=0, keepdims=True)
        sums[1, pl.ds(k, 1), :] = jnp.sum(dosage * dosage, axis=0, keepdims=True)
        sums[2, pl.ds(k, 1), :] = jnp.sum(jnp.where(called, 1.0, 0.0), axis=0, keepdims=True)
        return carry

    lax.fori_loop(0, blocks, local_sums, 0)

    @pl.when(jnp.logical_not(is_root))
    def _():
        sums_copy(col).start()

    @pl.when(is_root)
    def _():
        root_copy.wait()

    out_ref[...] = jnp.zeros_like(out_ref)
    factor = 1.0 / math.sqrt(blocks * variants)

    def standardize(values, k):
        center, scale = scaling[0, pl.ds(k, 1), :], scaling[1, pl.ds(k, 1), :]
        return jnp.where(values >= 0, (values - center) * scale, 0.0)

    def prepare_column(k):
        for held, place in ((own, row), (other, 1 - row)):
            first_part, second_part = split(standardize(held[k], k) * factor)
            spot = pl.ds(pl.multiple_of(place * samples, samples), samples)
            high[k, spot, :] = first_part
            low[k, spot, :] = second_part

    def prepare_row(c):
        k = c // PIECES
        spot = pl.ds(pl.multiple_of((c % PIECES) * piece, piece), piece)
        first_part, second_part = split(standardize(rows[k, spot, :], k))
        row_high[k, spot, :] = first_part
        row_low[k, spot, :] = second_part

    def product(left, right):
        return lax.dot_general(
            left, right, (((1,), (1,)), ((), ())), preferred_element_type=jnp.float32)

    def multiply(k, begin, end):
        left_high, left_low = row_high[k], row_low[k]
        right_high, right_low = high[k, begin:end, :], low[k, begin:end, :]
        out_ref[:, begin:end] += (
            product(left_high, right_high)
            + (product(left_low, right_high) + product(left_high, right_low)))

    width = out_ref.shape[1]

    def step(c, carry):
        @pl.when(jnp.logical_not(is_root))
        def _():
            forward(c, 0, parent).wait_recv()

            @pl.when(has_a)
            def _():
                forward(c, 0, child_a).start()

            @pl.when(has_b)
            def _():
                forward(c, 1, child_b).start()

            @pl.when(c == arrival)
            def _():
                totals_copy(0, parent).wait_recv()

                @pl.when(has_a)
                def _():
                    totals_copy(0, child_a).start()

                @pl.when(has_b)
                def _():
                    totals_copy(1, child_b).start()

        @pl.when(is_root)
        def _():
            from_root(c).wait_send()

            @pl.when(c + WINDOW < pieces)
            def _():
                from_root(c + WINDOW).start()

            @pl.when(c == GATHERED)
            def _():
                joined[...] = sums[...]

                def add(j, carry):
                    sums_copy(j).wait_recv()
                    joined[...] += gathered[j]
                    return carry

                lax.fori_loop(1, columns, add, 0)
                joined_copy.start()

            @pl.when(c == TOTALLED)
            def _():
                joined_copy.wait_recv()
                totals[...] = joined[...] + joined_in[...]
                totals_copy(0, child_a).start()

        @pl.when(c == arrival)
        def _():
            counts = jnp.maximum(totals[2], 1.0)
            center = totals[0] / counts
            spread = jnp.sqrt(jnp.maximum(totals[1] / counts - center * center, 0.05))
            scaling[0] = center
            scaling[1] = 1.0 / spread

        @pl.when(jnp.logical_and(c >= 1, c < 1 + blocks))
        def _():
            pair_copy(c - 1).start()

        since = c - arrival - 1

        @pl.when(jnp.logical_and(since >= 0, since < blocks))
        def _():
            pair_copy(since).wait_recv()
            prepare_column(since)

        for j in range(2):
            @pl.when(jnp.logical_and(since >= 0, 2 * since + j <= c))
            def _():
                prepare_row(2 * since + j)

        @pl.when(jnp.logical_and(since >= 0, c // 2 < since))
        def _():
            prepare_row(c)

        late = arrival + PIECES // 2
        for half in range(2):
            at = c - half
            caught = at // PIECES
            held = (at - late) // (PIECES // 2)
            on_time = jnp.logical_and(
                at % PIECES == PIECES - 1, at >= late + (PIECES // 2) * caught)
            was_held = jnp.logical_and(
                jnp.logical_and(at >= late, (at - late) % (PIECES // 2) == 0),
                at > PIECES * held + PIECES - 1)

            @pl.when(jnp.logical_and(jnp.logical_or(on_time, was_held), at < pieces - 1))
            def _():
                multiply(jnp.where(on_time, caught, held), half * width // 2,
                         (half + 1) * width // 2)

        return carry

    lax.fori_loop(0, pieces, step, 0)
    multiply(blocks - 1, 0, width)

    @pl.when(is_root)
    def _():
        joined_copy.wait_send()
        totals_copy(0, child_a).wait_send()

    @pl.when(jnp.logical_not(is_root))
    def _():
        sums_copy(col).wait_send()

        @pl.when(has_a)
        def _():
            totals_copy(0, child_a).wait_send()

        @pl.when(has_b)
        def _():
            totals_copy(1, child_b).wait_send()

    def drain_pair(k, carry):
        pair_copy(k).wait_send()
        return carry

    lax.fori_loop(0, blocks, drain_pair, 0)

    def drain(c, carry):
        @pl.when(jnp.logical_and(has_a, jnp.logical_not(is_root)))
        def _():
            forward(c, 0, child_a).wait_send()

        @pl.when(has_b)
        def _():
            forward(c, 1, child_b).wait_send()

        return carry

    lax.fori_loop(0, pieces, drain, 0)


def per_device(slow_n, fast_n, genotypes, prior_slab):
    blocks, samples, variants = genotypes.shape
    height, width = prior_slab.shape
    columns = slow_n * fast_n
    pieces = blocks * PIECES
    calls = pltpu.VMEM((blocks, samples, variants), jnp.float32)
    column_part = pltpu.VMEM((blocks, width, variants), jnp.bfloat16)
    row_part = pltpu.VMEM((blocks, samples, variants), jnp.bfloat16)
    sums = pltpu.VMEM((3, blocks, variants), jnp.float32)
    accumulated = pl.pallas_call(
        functools.partial(kernel, slow_n, fast_n),
        out_shape=jax.ShapeDtypeStruct((height, width), jnp.float32),
        in_specs=[pl.BlockSpec(memory_space=pl.ANY)],
        out_specs=pl.BlockSpec(memory_space=pltpu.VMEM),
        scratch_shapes=[
            calls, calls, calls, column_part, column_part, row_part, row_part,
            sums, pltpu.VMEM((columns, 3, blocks, variants), jnp.float32), sums, sums, sums,
            pltpu.VMEM((2, blocks, variants), jnp.float32),
            pltpu.SemaphoreType.DMA((2,)),
            pltpu.SemaphoreType.DMA((blocks,)),
            pltpu.SemaphoreType.DMA((blocks,)),
            pltpu.SemaphoreType.DMA,
            pltpu.SemaphoreType.DMA((columns,)),
            pltpu.SemaphoreType.DMA((2,)),
            pltpu.SemaphoreType.DMA((2,)),
            pltpu.SemaphoreType.DMA,
            pltpu.SemaphoreType.DMA((2, pieces)),
            pltpu.SemaphoreType.DMA((pieces,)),
        ],
        compiler_params=pltpu.CompilerParams(
            collective_id=0, has_side_effects=True, vmem_limit_bytes=VMEM_MIB * 2**20),
        cost_estimate=pl.CostEstimate(
            flops=6 * height * width * blocks * variants,
            bytes_accessed=4 * (blocks * samples * variants + height * width),
            transcendentals=0),
    )(genotypes)
    return prior_slab + accumulated


def solution(mesh):
    slow_n, fast_n = grid_of(mesh.shape["col"])
    placed = (P(None, ("grp", "col", "row"), None), P(("grp", "row"), "col"))
    return jax.shard_map(
        functools.partial(per_device, slow_n, fast_n), mesh=mesh, in_specs=placed,
        out_specs=P(("grp", "row"), "col"), check_vma=False
    )
```

time: 50 us -> 42.5 us (0.85)
  Pallas kernels: 45.9 us -> 41 us
  local copies, waits for them, and re-layouts: 3.95 us -> 0.01 us
  other arithmetic: 0 us -> 1.15 us
    pallas_call x1, Pallas kernels: 45.9 us -> 41 us  [per_device(): pl.pallas_call(functools.partial(kernel, slow_n, fast_n), out_shape=jax.S...]
    unnamed x5 -> x2, local copies, waits for them, and re-layouts: 3.95 us -> 0.01 us
    add x0 -> x1, other arithmetic: none -> 1.15 us  [per_device(): return prior_slab + accumulated]
where the time goes in v2:
time: 42.5 us; the launch traced here: 42.1 us
  Pallas kernels  41 us (96%)
  other arithmetic  1.15 us (3%)
    pallas_call x1, Pallas kernels, per_device(): pl.pallas_call(functools.partial(kernel, slow_n, fast_n), out_shape=jax.S...  41 us
    add x1, other arithmetic, per_device(): return prior_slab + accumulated  1.15 us

profile of v2, /device:TPU:26, one launch (start us, length us, event | category | flops | bytes accessed | tf_op | source)
XLA Modules:
  0.0 42.1 jit_solution(4914897113446249717)
XLA Ops:
  0.0 0.0 copy-start
  0.0 41.0 %shard_map.28 = f32[384,768]{1,0:T(8,128)S(1)} custom-call(f32[6,384,256]{2,1,0:T(8,128)} %calls_hbm.1), custom_call_target="tpu_custom_call" | custom-call | flops 2717908992 | bytes 3538944 | tf_op jit(solution)/shard_map/pallas_call | solution.py:331
  41.0 0.0 copy-done
  41.0 1.1 %add.3 = f32[384,768]{1,0:T(8,128)} add(f32[384,768]{1,0:T(8,128)S(1)} %copy-done, f32[384,768]{1,0:T(8,128)S(1)} %shard_map.28) | non-fusion elementwise | flops 294912 | bytes 3538944 | tf_op jit(solution)/shard_map/add | solution.py:358
Async XLA Ops:
  0.0 41.0 %copy-start = (f32[384,768]{1,0:T(8,128)S(1)}, f32[384,768]{1,0:T(8,128)}, u32[]{:S(2)}) copy-start(f32[384,768]{1,0:T(8,128)} %param.3) | copy-start | bytes 3538948

commit v3 on v2

--- a/solution.py
+++ b/solution.py
@@ -10,7 +10,7 @@
 
 MESH = pl.DeviceIdType.MESH
 PIECES = 8
-WINDOW = 8
+LATE = 3
 GATHERED = 7
 TOTALLED = 10
 VMEM_MIB = 52
@@ -28,15 +28,16 @@
 
 def kernel(slow_n, fast_n, calls_hbm, out_ref, own, other, rows, high, low, row_high, row_low,
            sums, gathered, joined, joined_in, totals, scaling, local_sem, pair_send, pair_recv,
-           sums_send, sums_recv, joined_sem, totals_send, totals_recv, piece_send, piece_recv):
+           sums_send, sums_recv, joined_sem, totals_send, totals_recv, root_send,
+           piece_send, piece_recv):
     blocks, samples, variants = own.shape
     columns = gathered.shape[0]
     piece = samples // PIECES
     pieces = blocks * PIECES
-    arrival = TOTALLED + WINDOW
+    arrival = TOTALLED + PIECES
 
     grp, col, row = lax.axis_index("grp"), lax.axis_index("col"), lax.axis_index("row")
-    z, x = col // fast_n, col % fast_n
+    z, x = lax.div(col, fast_n), lax.rem(col, fast_n)
     first, second = jnp.where(row == 0, z, x), jnp.where(row == 0, x, z)
     first_n = jnp.where(row == 0, slow_n, fast_n)
     second_n = jnp.where(row == 0, fast_n, slow_n)
@@ -66,9 +67,11 @@
 
     root = (grp, 0, row)
 
-    own_copy = pltpu.make_async_copy(calls_hbm, own, local_sem.at[0])
-    own_copy.start()
-    root_copy = pltpu.make_async_copy(calls_hbm, rows, local_sem.at[1])
+    def own_copy(k):
+        return pltpu.make_async_copy(calls_hbm.at[k], own.at[k], local_sem.at[k])
+
+    for k in range(blocks):
+        own_copy(k).start()
 
     barrier = pltpu.get_barrier_semaphore()
     pl.semaphore_signal(barrier, inc=1, device_id=pair, device_id_type=MESH)
@@ -89,22 +92,31 @@
         barrier,
         1 + jnp.where(is_root, 0, 1) + jnp.where(has_a, 1, 0) + jnp.where(has_b, 1, 0))
 
+    def place_of(c):
+        if isinstance(c, tuple):
+            return c
+        return lax.div(c, PIECES), lax.rem(c, PIECES)
+
+    def index_of(c):
+        return c[0] * PIECES + c[1] if isinstance(c, tuple) else c
+
     def part(ref, c):
-        return ref.at[c // PIECES, pl.ds(pl.multiple_of((c % PIECES) * piece, piece), piece)]
+        k, j = place_of(c)
+        return ref.at[k, pl.ds(pl.multiple_of(j * piece, piece), piece)]
 
     def from_root(c):
         return pltpu.make_async_remote_copy(
-            src_ref=part(calls_hbm, c), dst_ref=part(rows, c), send_sem=piece_send.at[0, c],
-            recv_sem=piece_recv.at[c], device_id=child_a, device_id_type=MESH)
+            src_ref=part(calls_hbm, c), dst_ref=part(rows, c), send_sem=root_send.at[index_of(c)],
+            recv_sem=piece_recv.at[index_of(c)], device_id=child_a, device_id_type=MESH)
 
     def forward(c, which, target):
         return pltpu.make_async_remote_copy(
-            src_ref=part(rows, c), dst_ref=part(rows, c), send_sem=piece_send.at[which, c],
-            recv_sem=piece_recv.at[c], device_id=target, device_id_type=MESH)
+            src_ref=part(rows, c), dst_ref=part(rows, c), send_sem=piece_send.at[which],
+            recv_sem=piece_recv.at[index_of(c)], device_id=target, device_id_type=MESH)
 
     def pair_copy(k):
         return pltpu.make_async_remote_copy(
-            src_ref=calls_hbm.at[k], dst_ref=other.at[k], send_sem=pair_send.at[k],
+            src_ref=calls_hbm.at[k], dst_ref=other.at[k], send_sem=pair_send,
             recv_sem=pair_recv.at[k], device_id=pair, device_id_type=MESH)
 
     def sums_copy(j):
@@ -123,13 +135,11 @@
 
     @pl.when(is_root)
     def _():
-        for c in range(min(WINDOW, pieces)):
-            from_root(c).start()
-        root_copy.start()
-
-    own_copy.wait()
+        for j in range(PIECES):
+            from_root((0, j)).start()
 
     def local_sums(k, carry):
+        own_copy(k).wait()
         values = own[k]
         called = values >= 0
         dosage = jnp.where(called, values, 0.0)
@@ -144,10 +154,6 @@
     def _():
         sums_copy(col).start()
 
-    @pl.when(is_root)
-    def _():
-        root_copy.wait()
-
     out_ref[...] = jnp.zeros_like(out_ref)
     factor = 1.0 / math.sqrt(blocks * variants)
 
@@ -163,37 +169,50 @@
             low[k, spot, :] = second_part
 
     def prepare_row(c):
-        k = c // PIECES
-        spot = pl.ds(pl.multiple_of((c % PIECES) * piece, piece), piece)
-        first_part, second_part = split(standardize(rows[k, spot, :], k))
-        row_high[k, spot, :] = first_part
-        row_low[k, spot, :] = second_part
+        k, j = place_of(c)
+        spot = pl.ds(pl.multiple_of(j * piece, piece), piece)
+
+        def prepare(held):
+            first_part, second_part = split(standardize(held[k, spot, :], k))
+            row_high[k, spot, :] = first_part
+            row_low[k, spot, :] = second_part
+
+        @pl.when(is_root)
+        def _():
+            prepare(own)
+
+        @pl.when(jnp.logical_not(is_root))
+        def _():
+            prepare(rows)
 
     def product(left, right):
         return lax.dot_general(
             left, right, (((1,), (1,)), ((), ())), preferred_element_type=jnp.float32)
 
-    def multiply(k, begin, end):
-        left_high, left_low = row_high[k], row_low[k]
+    def multiply(k, begin, end, top=0, bottom=samples):
+        left_high, left_low = row_high[k, top:bottom, :], row_low[k, top:bottom, :]
         right_high, right_low = high[k, begin:end, :], low[k, begin:end, :]
-        out_ref[:, begin:end] += (
+        out_ref[top:bottom, begin:end] += (
             product(left_high, right_high)
             + (product(left_low, right_high) + product(left_high, right_low)))
 
     width = out_ref.shape[1]
 
-    def step(c, carry):
+    def step(k, j):
+        c = k * PIECES + j
+        now = (k, j)
+
         @pl.when(jnp.logical_not(is_root))
         def _():
-            forward(c, 0, parent).wait_recv()
+            forward(now, 0, parent).wait_recv()
 
             @pl.when(has_a)
             def _():
-                forward(c, 0, child_a).start()
+                forward(now, 0, child_a).start()
 
             @pl.when(has_b)
             def _():
-                forward(c, 1, child_b).start()
+                forward(now, 1, child_b).start()
 
             @pl.when(c == arrival)
             def _():
@@ -209,11 +228,11 @@
 
         @pl.when(is_root)
         def _():
-            from_root(c).wait_send()
-
-            @pl.when(c + WINDOW < pieces)
-            def _():
-                from_root(c + WINDOW).start()
+            from_root(now).wait_send()
+
+            @pl.when(k + 1 < blocks)
+            def _():
+                from_root((k + 1, j)).start()
 
             @pl.when(c == GATHERED)
             def _():
@@ -257,30 +276,33 @@
             def _():
                 prepare_row(2 * since + j)
 
-        @pl.when(jnp.logical_and(since >= 0, c // 2 < since))
-        def _():
-            prepare_row(c)
-
-        late = arrival + PIECES // 2
+        @pl.when(jnp.logical_and(since >= 0, c < 2 * since))
+        def _():
+            prepare_row(now)
+
+        late = arrival + PIECES // 2 + LATE
+        steps = [max(late + b * (PIECES // 2), (b + 1) * PIECES - 1) for b in range(blocks - 1)]
         for half in range(2):
-            at = c - half
-            caught = at // PIECES
-            held = (at - late) // (PIECES // 2)
-            on_time = jnp.logical_and(
-                at % PIECES == PIECES - 1, at >= late + (PIECES // 2) * caught)
-            was_held = jnp.logical_and(
-                jnp.logical_and(at >= late, (at - late) % (PIECES // 2) == 0),
-                at > PIECES * held + PIECES - 1)
-
-            @pl.when(jnp.logical_and(jnp.logical_or(on_time, was_held), at < pieces - 1))
-            def _():
-                multiply(jnp.where(on_time, caught, held), half * width // 2,
-                         (half + 1) * width // 2)
-
-        return carry
-
-    lax.fori_loop(0, pieces, step, 0)
-    multiply(blocks - 1, 0, width)
+            chosen = [c == at + half for at in steps]
+
+            @pl.when(functools.reduce(jnp.logical_or, chosen))
+            def _():
+                b = sum(jnp.where(is_now, b, 0) for b, is_now in enumerate(chosen))
+                multiply(b, half * width // 2, (half + 1) * width // 2)
+
+        @pl.when(c == pieces - PIECES // 2)
+        def _():
+            multiply(blocks - 1, 0, width, 0, samples // 2)
+
+    def block_steps(k, carry):
+        def one(j, carry):
+            step(k, j)
+            return carry
+
+        return lax.fori_loop(0, PIECES, one, carry)
+
+    lax.fori_loop(0, blocks, block_steps, 0)
+    multiply(blocks - 1, 0, width, samples // 2, samples)
 
     @pl.when(is_root)
     def _():
@@ -299,24 +321,22 @@
         def _():
             totals_copy(1, child_b).wait_send()
 
-    def drain_pair(k, carry):
-        pair_copy(k).wait_send()
-        return carry
-
-    lax.fori_loop(0, blocks, drain_pair, 0)
-
-    def drain(c, carry):
-        @pl.when(jnp.logical_and(has_a, jnp.logical_not(is_root)))
-        def _():
-            forward(c, 0, child_a).wait_send()
-
-        @pl.when(has_b)
-        def _():
-            forward(c, 1, child_b).wait_send()
-
-        return carry
-
-    lax.fori_loop(0, pieces, drain, 0)
+    def all_sent(which, target):
+        return pltpu.make_async_remote_copy(
+            src_ref=rows, dst_ref=rows, send_sem=piece_send.at[which],
+            recv_sem=piece_recv.at[0], device_id=target, device_id_type=MESH)
+
+    pltpu.make_async_remote_copy(
+        src_ref=own, dst_ref=other, send_sem=pair_send, recv_sem=pair_recv.at[0],
+        device_id=pair, device_id_type=MESH).wait_send()
+
+    @pl.when(jnp.logical_and(has_a, jnp.logical_not(is_root)))
+    def _():
+        all_sent(0, child_a).wait_send()
+
+    @pl.when(has_b)
+    def _():
+        all_sent(1, child_b).wait_send()
 
 
 def per_device(slow_n, fast_n, genotypes, prior_slab):
@@ -337,15 +357,16 @@
             calls, calls, calls, column_part, column_part, row_part, row_part,
             sums, pltpu.VMEM((columns, 3, blocks, variants), jnp.float32), sums, sums, sums,
             pltpu.VMEM((2, blocks, variants), jnp.float32),
-            pltpu.SemaphoreType.DMA((2,)),
             pltpu.SemaphoreType.DMA((blocks,)),
+            pltpu.SemaphoreType.DMA,
             pltpu.SemaphoreType.DMA((blocks,)),
             pltpu.SemaphoreType.DMA,
             pltpu.SemaphoreType.DMA((columns,)),
             pltpu.SemaphoreType.DMA((2,)),
             pltpu.SemaphoreType.DMA((2,)),
             pltpu.SemaphoreType.DMA,
-            pltpu.SemaphoreType.DMA((2, pieces)),
+            pltpu.SemaphoreType.DMA((pieces,)),
+            pltpu.SemaphoreType.DMA((2,)),
             pltpu.SemaphoreType.DMA((pieces,)),
         ],
         compiler_params=pltpu.CompilerParams(

time: 42.5 us -> 40.7 us (0.958)
  Pallas kernels: 41 us -> 39.2 us
    pallas_call x1, Pallas kernels: 41 us -> 39.2 us  [per_device(): pl.pallas_call(functools.partial(kernel, slow_n, fast_n), out_shape=jax.S...]
where the time goes in v3:
time: 40.7 us; the launch traced here: 40.3 us
  Pallas kernels  39.2 us (96%)
  other arithmetic  1.15 us (3%)
    pallas_call x1, Pallas kernels, per_device(): pl.pallas_call(functools.partial(kernel, slow_n, fast_n), out_shape=jax.S...  39.2 us
    add x1, other arithmetic, per_device(): return prior_slab + accumulated  1.15 us

profile of v3, /device:TPU:26, one launch (start us, length us, event | category | flops | bytes accessed | tf_op | source)
XLA Modules:
  0.0 40.3 jit_solution(6249977205261746296)
XLA Ops:
  0.0 0.0 copy-start
  0.0 39.2 %shard_map.28 = f32[384,768]{1,0:T(8,128)S(1)} custom-call(f32[6,384,256]{2,1,0:T(8,128)} %calls_hbm.1), custom_call_target="tpu_custom_call" | custom-call | flops 2717908992 | bytes 3538944 | tf_op jit(solution)/shard_map/pallas_call | solution.py:351
  39.2 0.0 copy-done
  39.2 1.1 %add.3 = f32[384,768]{1,0:T(8,128)} add(f32[384,768]{1,0:T(8,128)S(1)} %copy-done, f32[384,768]{1,0:T(8,128)S(1)} %shard_map.28) | non-fusion elementwise | flops 294912 | bytes 3538944 | tf_op jit(solution)/shard_map/add | solution.py:379
Async XLA Ops:
  0.0 39.2 %copy-start = (f32[384,768]{1,0:T(8,128)S(1)}, f32[384,768]{1,0:T(8,128)}, u32[]{:S(2)}) copy-start(f32[384,768]{1,0:T(8,128)} %param.3) | copy-start | bytes 3538948

commit v4 on v3

--- a/solution.py
+++ b/solution.py
@@ -11,8 +11,8 @@
 MESH = pl.DeviceIdType.MESH
 PIECES = 8
 LATE = 3
-GATHERED = 7
-TOTALLED = 10
+GATHERED = 6
+TOTALLED = 9
 VMEM_MIB = 52
 
 
@@ -48,20 +48,30 @@
     is_root = col == 0
     on_edge = jnp.logical_and(first == 0, second > 0)
     on_spine = second == 0
+    on_line = jnp.logical_and(first > 0, second > 0)
+    skips = second_n >= 3
+    before = jnp.where(jnp.logical_and(skips, second == 1), 2,
+                       jnp.where(jnp.logical_and(skips, second == 2), 0, second - 1))
     parent = device(
         jnp.where(on_edge, 1, jnp.where(on_spine, jnp.maximum(first - 1, 0), first)),
-        jnp.where(on_edge, second, jnp.where(on_spine, 0, second - 1)),
+        jnp.where(on_edge, second, jnp.where(on_spine, 0, before)),
     )
     has_a = jnp.logical_and(
         jnp.logical_not(on_edge),
-        jnp.where(on_spine, first + 1 < first_n, second + 1 < second_n),
+        jnp.where(on_spine, first + 1 < first_n,
+                  jnp.logical_and(second + 1 < second_n,
+                                  jnp.logical_not(jnp.logical_and(skips, second == 1)))),
     )
     child_a = device(
         jnp.where(on_spine, jnp.minimum(first + 1, first_n - 1), first),
         jnp.where(on_spine, 0, jnp.minimum(second + 1, second_n - 1)),
     )
     has_b = jnp.where(on_spine, first >= 1, first == 1)
-    child_b = device(jnp.where(on_spine, first, 0), jnp.where(on_spine, 1, second))
+    child_b = device(
+        jnp.where(on_spine, first, 0),
+        jnp.where(on_spine, jnp.where(skips, 2, 1), second))
+    has_c = jnp.logical_and(jnp.logical_and(skips, on_line), second == 2)
+    child_c = device(first, jnp.minimum(1, second_n - 1))
 
     pair = (grp, col, 1 - row)
 
@@ -90,7 +100,8 @@
 
     pl.semaphore_wait(
         barrier,
-        1 + jnp.where(is_root, 0, 1) + jnp.where(has_a, 1, 0) + jnp.where(has_b, 1, 0))
+        1 + jnp.where(is_root, 0, 1) + jnp.where(has_a, 1, 0) + jnp.where(has_b, 1, 0)
+        + jnp.where(has_c, 1, 0))
 
     def place_of(c):
         if isinstance(c, tuple):
@@ -210,6 +221,10 @@
             def _():
                 forward(now, 0, child_a).start()
 
+            @pl.when(has_c)
+            def _():
+                forward(now, 2, child_c).start()
+
             @pl.when(has_b)
             def _():
                 forward(now, 1, child_b).start()
@@ -225,6 +240,10 @@
                 @pl.when(has_b)
                 def _():
                     totals_copy(1, child_b).start()
+
+                @pl.when(has_c)
+                def _():
+                    totals_copy(2, child_c).start()
 
         @pl.when(is_root)
         def _():
@@ -321,6 +340,10 @@
         def _():
             totals_copy(1, child_b).wait_send()
 
+        @pl.when(has_c)
+        def _():
+            totals_copy(2, child_c).wait_send()
+
     def all_sent(which, target):
         return pltpu.make_async_remote_copy(
             src_ref=rows, dst_ref=rows, send_sem=piece_send.at[which],
@@ -337,6 +360,10 @@
     @pl.when(has_b)
     def _():
         all_sent(1, child_b).wait_send()
+
+    @pl.when(has_c)
+    def _():
+        all_sent(2, child_c).wait_send()
 
 
 def per_device(slow_n, fast_n, genotypes, prior_slab):
@@ -363,10 +390,10 @@
             pltpu.SemaphoreType.DMA,
             pltpu.SemaphoreType.DMA((columns,)),
             pltpu.SemaphoreType.DMA((2,)),
-            pltpu.SemaphoreType.DMA((2,)),
+            pltpu.SemaphoreType.DMA((3,)),
             pltpu.SemaphoreType.DMA,
             pltpu.SemaphoreType.DMA((pieces,)),
-            pltpu.SemaphoreType.DMA((2,)),
+            pltpu.SemaphoreType.DMA((3,)),
             pltpu.SemaphoreType.DMA((pieces,)),
         ],
         compiler_params=pltpu.CompilerParams(

time: 40.7 us -> 40.5 us (level)
  no operation moved by 1% of the time
where the time goes in v4:
time: 40.5 us; the launch traced here: 40.4 us
  Pallas kernels  39.2 us (97%)
  other arithmetic  1.15 us (3%)
    pallas_call x1, Pallas kernels, per_device(): pl.pallas_call(functools.partial(kernel, slow_n, fast_n), out_shape=jax.S...  39.2 us
    add x1, other arithmetic, per_device(): return prior_slab + accumulated  1.15 us

profile of v4, /device:TPU:26, one launch (start us, length us, event | category | flops | bytes accessed | tf_op | source)
XLA Modules:
  0.0 40.4 jit_solution(1921185281132444901)
XLA Ops:
  0.0 0.0 copy-start
  0.0 39.2 %shard_map.28 = f32[384,768]{1,0:T(8,128)S(1)} custom-call(f32[6,384,256]{2,1,0:T(8,128)} %calls_hbm.1), custom_call_target="tpu_custom_call" | custom-call | flops 2717908992 | bytes 3538944 | tf_op jit(solution)/shard_map/pallas_call | solution.py:378
  39.2 0.0 copy-done
  39.2 1.1 %add.3 = f32[384,768]{1,0:T(8,128)} add(f32[384,768]{1,0:T(8,128)S(1)} %copy-done, f32[384,768]{1,0:T(8,128)S(1)} %shard_map.28) | non-fusion elementwise | flops 294912 | bytes 3538944 | tf_op jit(solution)/shard_map/add | solution.py:406
Async XLA Ops:
  0.0 39.2 %copy-start = (f32[384,768]{1,0:T(8,128)S(1)}, f32[384,768]{1,0:T(8,128)}, u32[]{:S(2)}) copy-start(f32[384,768]{1,0:T(8,128)} %param.3) | copy-start | bytes 3538948
